TPU v7x, 32 devices: a whole 2x2x4 slice. The times are simulated.
32 devices in a mesh: grp: 2 (over y), gx: 4 (over z), gy: 2 (over x), gz: 2 (over core).
Axes of the slice: x: 2, y: 2, z: 4, core: 2. Of those that a mesh axis runs over, the one named last changes fastest.
Arguments:
- ensemble: bfloat16 [128, 32, 32, 256], P(('grp', 'gx'), 'gy', 'gz'), parts along dimension 0, may hold values from -40 to 40
- wind_field: float32 [3, 128, 32, 32], P(None, ('grp', 'gx'), 'gy', 'gz'), parts along dimension 1, may hold values from -0.5 to 0.5
- obs_value: float32 [128, 32, 16], P(('grp', 'gx'), 'gy', 'gz'), parts along dimension 0, may hold values from -60 to 60
- obs_weight: float32 [128, 32, 16], P(('grp', 'gx'), 'gy', 'gz'), parts along dimension 0, may hold values from 0.1 to 1.75
- obs_cell: int32 [128, 32, 16], P(('grp', 'gx'), 'gy', 'gz'), parts along dimension 0, may hold values from 0 to 4095, as said below
- obs_used: int32 [128, 32, 16], P(('grp', 'gx'), 'gy', 'gz'), parts along dimension 0, may hold values 0 or 1
Outputs:
- analysis: bfloat16 [128, 32, 32, 256], P(('grp', 'gx'), 'gy', 'gz'), parts along dimension 0
There are 2 independent parts, one for each index of `grp`. A program takes and returns all parts, laid end to end along the dimension named above; each array names one. Nothing has to cross between parts.
Inputs may be any that keep to these rules, and one draw needn't show every extreme that they name: `obs_cell`: each entry names a cell of the grid block held by the same device, numbered (x * 16 + y) * 16 + z inside the block.
All inputs are finite; a program needn't handle non-finite values. No bound on the sum of `obs_used` on one device may be relied on, other than what follows from the above.
Results may differ from a plain program's by a relative error of at most 0.0067.
Values may be sent and summed in bfloat16 or wider, within the bound.
A program may use at most 64 MiB of HBM per device.

v0:
```python
import math

import jax
import jax.numpy as jnp
from jax import lax
from jax.sharding import PartitionSpec as P

ITERS = 5


diffusion = 0.1
steepen = 0.1


def padded_2(block, sides, width):
    for axis, dim in sides:
        count = lax.axis_size(axis)
        forward = [(i, i + 1) for i in range(count - 1)]
        backward = [(target, source) for source, target in forward]
        low = lax.ppermute(
            lax.slice_in_dim(block, block.shape[dim] - width, None, axis=dim), axis, forward
        )
        high = lax.ppermute(lax.slice_in_dim(block, 0, width, axis=dim), axis, backward)
        block = jnp.concatenate([low, block, high], axis=dim)
    return block


def advance(padded, wind_field):
    centre = padded[1:-1, 1:-1, 1:-1].astype(jnp.float32)
    ahead_x = padded[2:, 1:-1, 1:-1].astype(jnp.float32)
    behind_x = padded[:-2, 1:-1, 1:-1].astype(jnp.float32)
    ahead_y = padded[1:-1, 2:, 1:-1].astype(jnp.float32)
    behind_y = padded[1:-1, :-2, 1:-1].astype(jnp.float32)
    ahead_z = padded[1:-1, 1:-1, 2:].astype(jnp.float32)
    behind_z = padded[1:-1, 1:-1, :-2].astype(jnp.float32)
    laplace = ahead_x + behind_x + ahead_y + behind_y + ahead_z + behind_z - 6.0 * centre
    transport = (wind_field[0][..., None] + steepen * centre) * (ahead_x - behind_x)
    transport = transport + wind_field[1][..., None] * (ahead_y - behind_y)
    transport = transport + wind_field[2][..., None] * (ahead_z - behind_z)
    return lax.optimization_barrier(
        (centre + diffusion * laplace - 0.5 * transport).astype(jnp.bfloat16)
    )


def product(left, right):
    return jnp.dot(left, right, precision=lax.Precision.HIGHEST)


def inverse_root(gram_full):
    member_states = gram_full.shape[0]
    identity = jnp.eye(member_states, dtype=jnp.float32)
    coupled = identity + gram_full
    frob_norm = jnp.sqrt(jnp.sum(coupled * coupled))
    iterate_y = coupled / frob_norm
    iterate_z = identity
    for sweep in range(ITERS):
        factor_p = 0.5 * (3.0 * identity - product(iterate_z, iterate_y))
        iterate_y = product(factor_p, iterate_y)
        iterate_z = product(factor_p, iterate_z)
    return iterate_z / jnp.sqrt(frob_norm)


def per_device(ensemble, wind_field, obs_value, obs_weight, obs_cell, obs_used):
    extent_x, extent_y, extent_z, member_states = ensemble.shape

    def advance_border(field):
        padded = padded_2(field, (("gx", 0), ("gy", 1), ("gz", 2)), 1)
        return advance(padded, wind_field)

    predicted_state = advance_border(advance_border(ensemble))
    ensemble_average = jnp.mean(predicted_state.astype(jnp.float32), axis=3)
    member_departures = (predicted_state.astype(jnp.float32) - ensemble_average[..., None]).astype(
        jnp.bfloat16
    )
    flat_anom = member_departures.reshape(-1, member_states)
    mean_flat = ensemble_average.reshape(-1)
    obs_spots = obs_cell.reshape(-1)
    picked = jnp.take(flat_anom, obs_spots, axis=0)
    mean_at = jnp.take(mean_flat, obs_spots, axis=0)
    obs_total = obs_cell.size * lax.axis_size("gx") * lax.axis_size("gy") * lax.axis_size("gz")
    in_use = obs_used.reshape(-1).astype(jnp.float32)
    obs_scale = obs_weight.reshape(-1)
    values = obs_value.reshape(-1)
    scaled = (
        (in_use * obs_scale / math.sqrt(obs_total))[:, None] * picked.astype(jnp.float32)
    ).astype(jnp.bfloat16)
    innovation = (in_use * obs_scale * (values - mean_at) / math.sqrt(obs_total)).astype(
        jnp.bfloat16
    )
    gram_part = lax.dot_general(
        scaled, scaled, (((0,), (0,)), ((), ())), preferred_element_type=jnp.float32
    )
    couple_part = jnp.dot(innovation, scaled, preferred_element_type=jnp.float32)
    gram_full, coupling = lax.psum((gram_part, couple_part), ("gx", "gy", "gz"))
    transform = inverse_root(gram_full)
    shift = product(transform, product(transform, coupling))
    weights = (transform + shift[:, None]).astype(jnp.bfloat16)
    mixed = jnp.dot(flat_anom, weights, preferred_element_type=jnp.float32)
    analysis = (mean_flat[:, None] + mixed).astype(jnp.bfloat16)
    return analysis.reshape(extent_x, extent_y, extent_z, member_states)


def solution(mesh):
    in_specs = (
        P(("grp", "gx"), "gy", "gz", None),
        P(None, ("grp", "gx"), "gy", "gz"),
        P(("grp", "gx"), "gy", "gz"),
        P(("grp", "gx"), "gy", "gz"),
        P(("grp", "gx"), "gy", "gz"),
        P(("grp", "gx"), "gy", "gz"),
    )
    out_specs = P(("grp", "gx"), "gy", "gz", None)
    return jax.shard_map(
        per_device, mesh=mesh, in_specs=in_specs, out_specs=out_specs, check_vma=False
    )
```

profile of v0, /device:TPU:0, one launch (start us, length us, event | category | flops | bytes accessed | tf_op | source)
XLA Modules:
  0.0 221.3 jit_solution(8572135581183431103)
XLA Ops:
  7.5 4.9 %collective-permute-start.1 = (bf16[1,16,16,256]{3,2,1,0:T(8,128)(2,1)S(1)}, bf16[1,16,16,256]{3,2,1,0:T(8,128)(2,1)S(1)}, u32[]{:S(2)}, u32[]{:S(2)}) collective-permute-start(bf16[1,16,16,256]{3,2,1,0:T(8,128)(2,1)S(1)} %get-tuple-element.18), channel_id=1, source_target_pairs={{0,4},{4,8},{8,12},{1,5},{5,9},{9,13},{2,6},{6,10},{10,14},{3,7},{... | collective-permute-start | bytes 393224 | tf_op jit(solution)/shard_map/ppermute | solution.py:20
  13.8 1.4 collective-permute-done.1
  15.2 1.8 constant_dynamic-update-slice_fusion.1
  17.1 2.3 %collective-permute-done = bf16[1,16,16,256]{3,2,1,0:T(8,128)(2,1)S(1)} collective-permute-done((bf16[1,16,16,256]{3,2,1,0:T(8,128)(2,1)S(1)}, bf16[1,16,16,256]{3,2,1,0:T(8,128)(2,1)S(1)}, u32[]{:S(2)}, u32[]{:S(2)}) %collective-permute-start) | collective-permute-done | bytes 131104 | tf_op jit(solution)/shard_map/ppermute | solution.py:23
  19.4 1.3 collective-permute-start.2
  20.7 4.6 %collective-permute-start.3 = (bf16[18,1,16,256]{3,2,1,0:T(8,128)(2,1)S(1)}, bf16[18,1,16,256]{3,2,1,0:T(8,128)(2,1)S(1)}, u32[]{:S(2)}, u32[]{:S(2)}) collective-permute-start(bf16[18,1,16,256]{3,2,1,0:T(8,128)(2,1)S(1)} %get-tuple-element.13), channel_id=1, source_target_pairs={{0,2},{1,3},{4,6},{5,7},{8,10},{9,11},{12,14},{13,15},{16,18},{17,... | collective-permute-start | bytes 442376 | tf_op jit(solution)/shard_map/ppermute | solution.py:20
  26.4 1.5 collective-permute-done.3
  29.8 3.2 %collective-permute-start.5 = (bf16[18,18,1,256]{3,1,2,0:T(8,128)(2,1)S(1)}, bf16[18,18,1,256]{3,1,2,0:T(8,128)(2,1)S(1)}, u32[]{:S(2)}, u32[]{:S(2)}) collective-permute-start(bf16[18,18,1,256]{3,1,2,0:T(8,128)(2,1)S(1)} %copy.42), channel_id=1, source_target_pairs={{0,1},{2,3},{4,5},{6,7},{8,9},{10,11},{12,13},{14,15},{16,17},{18,... | collective-permute-start | bytes 497672 | tf_op jit(solution)/shard_map/ppermute | solution.py:20
  34.7 10.0 %fusion.6 = bf16[16,16,16,256]{3,2,1,0:T(8,128)(2,1)S(1)} fusion(bf16[16,16,16,256]{3,2,1,0:T(8,128)(2,1)S(1)} %copy-done.3, bf16[18,18,1,256]{3,2,1,0:T(2,128)(2,1)S(1)} %copy.43, bf16[18,1,16,256]{3,2,1,0:T(8,128)(2,1)S(1)} %collective-permute-done.2, bf16[18,16,16,256]{3,2,1,0:T(8,128)(2,1)S(1)} %copy-done.2, ...), kind=kLoop, calls=%fused_computation.33 | loop fusion | flops 57671680 | bytes 7491584 | tf_op jit(solution)/shard_map/convert_element_type | solution.py:41
  46.0 4.6 %collective-permute-start.7 = (bf16[1,16,16,256]{3,2,1,0:T(8,128)(2,1)S(1)}, bf16[1,16,16,256]{3,2,1,0:T(8,128)(2,1)S(1)}, u32[]{:S(2)}, u32[]{:S(2)}) collective-permute-start(bf16[1,16,16,256]{3,2,1,0:T(8,128)(2,1)S(1)} %get-tuple-element.15), channel_id=1, source_target_pairs={{0,4},{4,8},{8,12},{1,5},{5,9},{9,13},{2,6},{6,10},{10,14},{3,7},{... | collective-permute-start | bytes 393224 | tf_op jit(solution)/shard_map/ppermute | solution.py:20
  50.7 1.4 collective-permute-done.6
  54.6 4.6 %collective-permute-start.9 = (bf16[18,1,16,256]{3,2,1,0:T(8,128)(2,1)S(1)}, bf16[18,1,16,256]{3,2,1,0:T(8,128)(2,1)S(1)}, u32[]{:S(2)}, u32[]{:S(2)}) collective-permute-start(bf16[18,1,16,256]{3,2,1,0:T(8,128)(2,1)S(1)} %get-tuple-element.11), channel_id=1, source_target_pairs={{0,2},{1,3},{4,6},{5,7},{8,10},{9,11},{12,14},{13,15},{16,18},{17,... | collective-permute-start | bytes 442376 | tf_op jit(solution)/shard_map/ppermute | solution.py:20
  63.9 3.1 %collective-permute-start.11 = (bf16[18,18,1,256]{3,1,2,0:T(8,128)(2,1)S(1)}, bf16[18,18,1,256]{3,1,2,0:T(8,128)(2,1)S(1)}, u32[]{:S(2)}, u32[]{:S(2)}) collective-permute-start(bf16[18,18,1,256]{3,1,2,0:T(8,128)(2,1)S(1)} %copy.46), channel_id=1, source_target_pairs={{0,1},{2,3},{4,5},{6,7},{8,9},{10,11},{12,13},{14,15},{16,17},{18,... | collective-permute-start | bytes 497672 | tf_op jit(solution)/shard_map/ppermute | solution.py:20
  68.3 13.7 %fusion.16 = bf16[16,16,16,256]{3,2,1,0:T(8,128)(2,1)S(1)} fusion(bf16[16,16,16,256]{3,2,1,0:T(8,128)(2,1)S(1)} %fusion.6, bf16[18,18,1,256]{3,2,1,0:T(2,128)(2,1)S(1)} %copy.47, bf16[18,1,16,256]{3,2,1,0:T(8,128)(2,1)S(1)} %collective-permute-done.8, bf16[18,1,16,256]{3,2,1,0:T(8,128)(2,1)S(1)} %collective-permute-done.9, ...), kind=kLoop, calls=%fused_computation.43 | loop fusion | flops 74448896 | bytes 5132288 | tf_op jit(solution)/shard_map/convert_element_type | solution.py:41
  82.0 1.3 copy-done
  84.1 1.9 fusion.21
  86.2 9.1 %gather_fusion = bf16[2048,256]{1,0:T(8,128)(2,1)} fusion(bf16[4096,256]{1,0:T(8,128)(2,1)S(1)} %bitcast.48, s32[2048]{0:T(1024)S(1)} %broadcast_clamp_fusion), kind=kCustom, calls=%fused_computation | custom fusion | bytes 2105344 | tf_op jit(solution)/shard_map/jit(_take)/gather | solution.py:78
  95.2 11.8 %gather_fusion.1 = f32[2048]{0:T(1024)S(1)} fusion(f32[4096]{0:T(1024)S(1)} %div.28, s32[2048]{0:T(1024)S(1)} %broadcast_clamp_fusion), kind=kCustom, calls=%fused_computation.1 | custom fusion | bytes 24576 | tf_op jit(solution)/shard_map/jit(_take)/gather | solution.py:79
  107.0 1.8 multiply_convert_fusion
  110.3 36.1 %psum.15 = f32[256]{0:T(256)S(1)} all-reduce(f32[256]{0:T(256)S(1)} %bitcast.53), channel_id=1, replica_groups=mesh['grp'=2,'gx'=4,'gy'=2,'gz'=2] {'gx','gy','gz'}, use_global_device_ids=true, to_apply=%region_3.4 | all-reduce | flops 256 | bytes 2048 | tf_op jit(solution)/shard_map/psum | solution.py:94
  146.3 55.9 %all-reduce.2.cloned.1.call-done = f32[256,256]{1,0:T(8,128)} async-done(((f32[256,256]{1,0:T(8,128)}), f32[256,256]{1,0:T(8,128)}) %all-reduce.2.cloned.1.call-update) | async-done | bytes 262160 | tf_op jit(solution)/shard_map/psum | solution.py:94
  202.2 1.6 multiply_reduce_fusion
  206.1 1.4 fusion.32
  212.4 2.1 fusion
  (75 shorter events, 25.6 us)
Async XLA Ops:
  6.5 195.7 %all-reduce.2.cloned.1.call-start = ((), (), s32[]{:S(2)}) async-start(), calls=%async_computation | async-start | bytes 524288 | tf_op jit(solution)/shard_map/psum | solution.py:94
  7.5 7.7 %collective-permute-start.1 = (bf16[1,16,16,256]{3,2,1,0:T(8,128)(2,1)S(1)}, bf16[1,16,16,256]{3,2,1,0:T(8,128)(2,1)S(1)}, u32[]{:S(2)}, u32[]{:S(2)}) collective-permute-start(bf16[1,16,16,256]{3,2,1,0:T(8,128)(2,1)S(1)} %get-tuple-element.18), channel_id=1, source_target_pairs={{0,4},{4,8},{8,12},{1,5},{5,9},{9,13},{2,6},{6,10},{10,14},{3,7},{... | collective-permute-start | bytes 393224 | tf_op jit(solution)/shard_map/ppermute | solution.py:20
  12.5 6.9 %collective-permute-start = (bf16[1,16,16,256]{3,2,1,0:T(8,128)(2,1)S(1)}, bf16[1,16,16,256]{3,2,1,0:T(8,128)(2,1)S(1)}, u32[]{:S(2)}, u32[]{:S(2)}) collective-permute-start(bf16[1,16,16,256]{3,2,1,0:T(8,128)(2,1)S(1)} %get-tuple-element.17), channel_id=1, source_target_pairs={{4,0},{8,4},{12,8},{5,1},{9,5},{13,9},{6,2},{10,6},{14,10},{7,3},{... | collective-permute-start | bytes 393224 | tf_op jit(solution)/shard_map/ppermute | solution.py:23
  15.2 10.0 %copy-start.4 = (s32[16,16,8]{1,2,0:T(8,128)S(1)}, s32[16,16,8]{1,2,0:T(8,128)}, u32[]{:S(2)}) copy-start(s32[16,16,8]{1,2,0:T(8,128)} %param.10) | copy-start | bytes 24580
  19.3 9.1 %copy-start.1 = (bf16[18,16,16,256]{3,2,1,0:T(8,128)(2,1)}, bf16[18,16,16,256]{3,2,1,0:T(8,128)(2,1)S(1)}, u32[]{:S(2)}) copy-start(bf16[18,16,16,256]{3,2,1,0:T(8,128)(2,1)S(1)} %constant_dynamic-update-slice_fusion) | copy-start | bytes 7077892
  19.4 7.0 %collective-permute-start.2 = (bf16[18,1,16,256]{3,2,1,0:T(8,128)(2,1)S(1)}, bf16[18,1,16,256]{3,2,1,0:T(8,128)(2,1)S(1)}, u32[]{:S(2)}, u32[]{:S(2)}) collective-permute-start(bf16[18,1,16,256]{3,2,1,0:T(8,128)(2,1)S(1)} %get-tuple-element.14), channel_id=1, source_target_pairs={{2,0},{3,1},{6,4},{7,5},{10,8},{11,9},{14,12},{15,13},{18,16},{19,... | collective-permute-start | bytes 442376 | tf_op jit(solution)/shard_map/ppermute | solution.py:23
  20.7 7.2 %collective-permute-start.3 = (bf16[18,1,16,256]{3,2,1,0:T(8,128)(2,1)S(1)}, bf16[18,1,16,256]{3,2,1,0:T(8,128)(2,1)S(1)}, u32[]{:S(2)}, u32[]{:S(2)}) collective-permute-start(bf16[18,1,16,256]{3,2,1,0:T(8,128)(2,1)S(1)} %get-tuple-element.13), channel_id=1, source_target_pairs={{0,2},{1,3},{4,6},{5,7},{8,10},{9,11},{12,14},{13,15},{16,18},{17,... | collective-permute-start | bytes 442376 | tf_op jit(solution)/shard_map/ppermute | solution.py:20
  25.5 9.2 %copy-start.3 = (bf16[16,16,16,256]{3,2,1,0:T(8,128)(2,1)S(1)}, bf16[16,16,16,256]{3,2,1,0:T(8,128)(2,1)}, u32[]{:S(2)}) copy-start(bf16[16,16,16,256]{3,2,1,0:T(8,128)(2,1)} %param.6) | copy-start | bytes 6291460
  28.5 5.6 %collective-permute-start.4 = (bf16[18,18,1,256]{3,1,2,0:T(8,128)(2,1)S(1)}, bf16[18,18,1,256]{3,1,2,0:T(8,128)(2,1)S(1)}, u32[]{:S(2)}, u32[]{:S(2)}) collective-permute-start(bf16[18,18,1,256]{3,1,2,0:T(8,128)(2,1)S(1)} %copy.40), channel_id=1, source_target_pairs={{1,0},{3,2},{5,4},{7,6},{9,8},{11,10},{13,12},{15,14},{17,16},{19,... | collective-permute-start | bytes 497672 | tf_op jit(solution)/shard_map/ppermute | solution.py:23
  29.8 4.9 %copy-start.2 = (bf16[18,16,16,256]{3,2,1,0:T(8,128)(2,1)S(1)}, bf16[18,16,16,256]{3,2,1,0:T(8,128)(2,1)}, u32[]{:S(2)}) copy-start(bf16[18,16,16,256]{3,2,1,0:T(8,128)(2,1)} %copy-done.1) | copy-start | bytes 7077892
  29.8 4.5 %collective-permute-start.5 = (bf16[18,18,1,256]{3,1,2,0:T(8,128)(2,1)S(1)}, bf16[18,18,1,256]{3,1,2,0:T(8,128)(2,1)S(1)}, u32[]{:S(2)}, u32[]{:S(2)}) collective-permute-start(bf16[18,18,1,256]{3,1,2,0:T(8,128)(2,1)S(1)} %copy.42), channel_id=1, source_target_pairs={{0,1},{2,3},{4,5},{6,7},{8,9},{10,11},{12,13},{14,15},{16,17},{18,... | collective-permute-start | bytes 497672 | tf_op jit(solution)/shard_map/ppermute | solution.py:20
  44.7 7.4 %collective-permute-start.6 = (bf16[1,16,16,256]{3,2,1,0:T(8,128)(2,1)S(1)}, bf16[1,16,16,256]{3,2,1,0:T(8,128)(2,1)S(1)}, u32[]{:S(2)}, u32[]{:S(2)}) collective-permute-start(bf16[1,16,16,256]{3,2,1,0:T(8,128)(2,1)S(1)} %get-tuple-element.16), channel_id=1, source_target_pairs={{4,0},{8,4},{12,8},{5,1},{9,5},{13,9},{6,2},{10,6},{14,10},{7,3},{... | collective-permute-start | bytes 393224 | tf_op jit(solution)/shard_map/ppermute | solution.py:23
  46.0 7.3 %collective-permute-start.7 = (bf16[1,16,16,256]{3,2,1,0:T(8,128)(2,1)S(1)}, bf16[1,16,16,256]{3,2,1,0:T(8,128)(2,1)S(1)}, u32[]{:S(2)}, u32[]{:S(2)}) collective-permute-start(bf16[1,16,16,256]{3,2,1,0:T(8,128)(2,1)S(1)} %get-tuple-element.15), channel_id=1, source_target_pairs={{0,4},{4,8},{8,12},{1,5},{5,9},{9,13},{2,6},{6,10},{10,14},{3,7},{... | collective-permute-start | bytes 393224 | tf_op jit(solution)/shard_map/ppermute | solution.py:20
  53.3 8.0 %collective-permute-start.8 = (bf16[18,1,16,256]{3,2,1,0:T(8,128)(2,1)S(1)}, bf16[18,1,16,256]{3,2,1,0:T(8,128)(2,1)S(1)}, u32[]{:S(2)}, u32[]{:S(2)}) collective-permute-start(bf16[18,1,16,256]{3,2,1,0:T(8,128)(2,1)S(1)} %get-tuple-element.12), channel_id=1, source_target_pairs={{2,0},{3,1},{6,4},{7,5},{10,8},{11,9},{14,12},{15,13},{18,16},{19,... | collective-permute-start | bytes 442376 | tf_op jit(solution)/shard_map/ppermute | solution.py:23
  54.6 7.2 %collective-permute-start.9 = (bf16[18,1,16,256]{3,2,1,0:T(8,128)(2,1)S(1)}, bf16[18,1,16,256]{3,2,1,0:T(8,128)(2,1)S(1)}, u32[]{:S(2)}, u32[]{:S(2)}) collective-permute-start(bf16[18,1,16,256]{3,2,1,0:T(8,128)(2,1)S(1)} %get-tuple-element.11), channel_id=1, source_target_pairs={{0,2},{1,3},{4,6},{5,7},{8,10},{9,11},{12,14},{13,15},{16,18},{17,... | collective-permute-start | bytes 442376 | tf_op jit(solution)/shard_map/ppermute | solution.py:20
  62.6 4.4 %collective-permute-start.10 = (bf16[18,18,1,256]{3,1,2,0:T(8,128)(2,1)S(1)}, bf16[18,18,1,256]{3,1,2,0:T(8,128)(2,1)S(1)}, u32[]{:S(2)}, u32[]{:S(2)}) collective-permute-start(bf16[18,18,1,256]{3,1,2,0:T(8,128)(2,1)S(1)} %copy.44), channel_id=1, source_target_pairs={{1,0},{3,2},{5,4},{7,6},{9,8},{11,10},{13,12},{15,14},{17,16},{19,... | collective-permute-start | bytes 497672 | tf_op jit(solution)/shard_map/ppermute | solution.py:23
  63.9 4.1 %collective-permute-start.11 = (bf16[18,18,1,256]{3,1,2,0:T(8,128)(2,1)S(1)}, bf16[18,18,1,256]{3,1,2,0:T(8,128)(2,1)S(1)}, u32[]{:S(2)}, u32[]{:S(2)}) collective-permute-start(bf16[18,18,1,256]{3,1,2,0:T(8,128)(2,1)S(1)} %copy.46), channel_id=1, source_target_pairs={{0,1},{2,3},{4,5},{6,7},{8,9},{10,11},{12,13},{14,15},{16,17},{18,... | collective-permute-start | bytes 497672 | tf_op jit(solution)/shard_map/ppermute | solution.py:20
  82.0 1.3 copy-start
Sparse Core Ops, SparseCore 0:
  110.1 92.0 all-reduce.1
where the time goes:
time: 222 us; the launch traced here: 221 us
  waiting for transfers between devices  65.8 us (30%)
  blocking collectives  36.1 us (16%)
  starting transfers between devices  32.6 us (15%)
  other arithmetic  31.8 us (14%)
  local copies, waits for them, and re-layouts  29.1 us (13%)
  between operations  14.7 us (7%)
  matrix products  11.2 us (5%)
    psum x1, waiting for transfers between devices, per_device(): gram_full, coupling = lax.psum((gram_part, couple_part), ('gx', 'gy', 'gz'))  55.9 us
    psum x1, blocking collectives, per_device(): gram_full, coupling = lax.psum((gram_part, couple_part), ('gx', 'gy', 'gz'))  36.1 us
    ppermute x6, starting transfers between devices, padded_2(): lax.ppermute(lax.slice_in_dim(block, block.shape[dim] - width, None, axis...  24.8 us
    convert_element_type x2, other arithmetic, advance(): (centre + diffusion * laplace - 0.5 * transport).astype(jnp.bfloat16)  23.6 us
    gather x1, local copies, waits for them, and re-layouts, per_device(): mean_at = jnp.take(mean_flat, obs_spots, axis=0)  11.8 us
    gather x1, local copies, waits for them, and re-layouts, per_device(): picked = jnp.take(flat_anom, obs_spots, axis=0)  9.06 us
    ppermute x6, starting transfers between devices, padded_2(): lax.ppermute(lax.slice_in_dim(block, 0, width, axis=dim), axis, backward)  7.75 us
    dot_general x16, matrix products, product(): return jnp.dot(left, right, precision=lax.Precision.HIGHEST)  7.69 us
  transfers between devices with their start and end apart: 13, of which 9 were waited for; matrix products, arithmetic and copies ran while one was open for 3% of the time, Pallas kernels for 0%

commit v1 on v0

v1 whole, which is shorter than its diff:
```python
import functools

import jax
import jax.numpy as jnp
from jax import lax
from jax.experimental import pallas as pl
from jax.experimental.pallas import tpu as pltpu
from jax.sharding import PartitionSpec as P

ITERS = 5
DIFFUSION = 0.1
STEEPEN = 0.1
GRID_AXES = ("gx", "gy", "gz")
MESH = pl.DeviceIdType.MESH
F32 = jnp.float32
BF16 = jnp.bfloat16
VMEM = functools.partial(pl.BlockSpec, memory_space=pltpu.VMEM)
VMEM_LIMIT = 56 * 1024 * 1024


def product(left, right):
    return jnp.dot(left, right, precision=lax.Precision.HIGHEST, preferred_element_type=F32)


def contract(left, right, dims):
    return lax.dot_general(left, right, (dims, ((), ())), preferred_element_type=F32)


def collect_row(faces, y, piece, row):
    shift = (y % 8 - row) % 8
    moved = pltpu.roll(piece, shift, 0) if shift else piece
    rows = lax.broadcasted_iota(jnp.int32, piece.shape, 0)
    faces[y // 8] = moved if faces[y // 8] is None else jnp.where(rows == y % 8, moved, faces[y // 8])


def forecast_kernel(
    counts, ens, wind, spot_xz, spot_y, obs_sq, obs_sv,
    f_out, gram_out, coup_out,
    pad_a, pad_b, halo_z, in_x, in_y, in_z, out_x, out_y, out_z,
    obs_acc, root_w, pull_v, scaled, gram, send_sem, recv_sem,
):
    cx, cy, cz, members = ens.shape
    half = members // 2
    pos = [lax.axis_index(a) for a in GRID_AXES]
    has = [(pos[a] > 0, pos[a] < counts[a] - 1) for a in range(3)]
    inbox = (in_x, in_y, in_z)

    def target(a, d):
        where = pos[a] + (1 if d else counts[a] - 1)
        return {GRID_AXES[a]: lax.rem(where, counts[a])}

    def link(step, a, d):
        if a == 0:
            src = ens.at[(cx - 1) * d] if step == 0 else out_x.at[d]
        elif a == 1:
            src = ens.at[:, (cy - 1) * d] if step == 0 else out_y.at[d]
        else:
            src = out_z.at[step, d]
        return pltpu.make_async_remote_copy(
            src_ref=src,
            dst_ref=inbox[a].at[step, 1 - d],
            send_sem=send_sem.at[step, a, d],
            recv_sem=recv_sem.at[step, a, 1 - d],
            device_id=target(a, d),
            device_id_type=MESH,
        )

    def send(step, a):
        for d in range(2):
            @pl.when(has[a][d])
            def _():
                link(step, a, d).start()

    def receive(step, a, pad):
        for side in range(2):
            def border(values, a=a, side=side):
                if a == 0:
                    pad[(cx + 1) * side, 1 : cy + 1] = values
                elif a == 1:
                    pad[1 : cx + 1, (cy + 1) * side] = values
                else:
                    halo_z[side] = values

            @pl.when(has[a][side])
            def _():
                link(step, a, 1 - side).wait_recv()
                border(inbox[a][step, side].astype(F32))

            @pl.when(jnp.logical_not(has[a][side]))
            def _():
                border(jnp.zeros(inbox[a].shape[2:], F32))

    barrier = pltpu.get_barrier_semaphore()
    for a in range(3):
        for d in range(2):
            @pl.when(has[a][d])
            def _():
                pl.semaphore_signal(barrier, inc=1, device_id=target(a, d), device_id_type=MESH)
    neighbours = sum(has[a][d].astype(jnp.int32) for a in range(3) for d in range(2))
    pl.semaphore_wait(barrier, neighbours)

    send(0, 0)
    send(0, 1)

    def store_faces(step, x, first, last):
        out_z[step, 0, x] = jnp.concatenate(first, axis=0).astype(BF16)
        out_z[step, 1, x] = jnp.concatenate(last, axis=0).astype(BF16)

    def widen(x, carry):
        first, last = [None] * (cy // 8), [None] * (cy // 8)
        for y in range(cy):
            v = ens[x, y].astype(F32)
            pad_a[x + 1, y + 1] = v
            collect_row(first, y, v[:8], 0)
            collect_row(last, y, v[cz - 8 :], 7)
        store_faces(0, x, first, last)
        return carry

    lax.fori_loop(0, cx, widen, 0)
    send(0, 2)

    obs_acc[...] = jnp.zeros_like(obs_acc)
    chunks, chunk = spot_xz.shape

    def scatter(i, carry):
        row = pl.ds(i, 1)
        at_xz = lax.broadcasted_iota(jnp.int32, (cx * cz, chunk), 0) == spot_xz[row, :]
        at_y = lax.broadcasted_iota(jnp.int32, (cy, chunk), 0) == spot_y[row, :]
        parts = []
        for rest in (obs_sq[row, :], obs_sv[row, :]):
            for _ in range(3):
                part = rest.astype(BF16).astype(F32)
                parts.append(jnp.where(at_y, part, 0.0))
                rest = rest - part
        weighted = jnp.concatenate(parts, axis=0).astype(BF16)
        obs_acc[...] += contract(
            jnp.where(at_xz, 1.0, 0.0).astype(BF16), weighted, ((1,), (1,))
        )
        return carry

    lax.fori_loop(0, chunks, scatter, 0)
    sums = obs_acc[...]
    w_sum = sums[:, :cy] + sums[:, cy : 2 * cy] + sums[:, 2 * cy : 3 * cy]
    v_sum = sums[:, 3 * cy : 4 * cy] + sums[:, 4 * cy : 5 * cy] + sums[:, 5 * cy :]
    root_w[...] = jnp.sqrt(w_sum).reshape(cx, cz, cy)
    pull_v[...] = v_sum.reshape(cx, cz, cy)

    top = lax.broadcasted_iota(jnp.int32, (8, members), 0) == 0
    bottom = lax.broadcasted_iota(jnp.int32, (8, members), 0) == 7
    pieces = cz // 8

    def advance_row(pad, x, y):
        def rows(i, j):
            return [pad[i, j, 8 * k : 8 * k + 8] for k in range(pieces)]

        centre = rows(x + 1, y + 1)
        x_up, x_dn = rows(x + 2, y + 1), rows(x, y + 1)
        y_up, y_dn = rows(x + 1, y + 2), rows(x + 1, y)
        below = jnp.broadcast_to(halo_z[0, x, y : y + 1, :], (8, members))
        above = jnp.broadcast_to(halo_z[1, x, y : y + 1, :], (8, members))
        rolled_up = [pltpu.roll(c, 7, 0) for c in centre] + [above]
        rolled_dn = [below] + [pltpu.roll(c, 1, 0) for c in centre]
        result = []
        for k in range(pieces):
            c = centre[k]
            z_up = jnp.where(bottom, rolled_up[k + 1], rolled_up[k])
            z_dn = jnp.where(top, rolled_dn[k], rolled_dn[k + 1])
            wx, wy, wz = (wind[i, x, 8 * k : 8 * k + 8, y : y + 1] for i in range(3))
            laplace = ((x_up[k] + x_dn[k]) + (y_up[k] + y_dn[k])) + ((z_up + z_dn) - 6.0 * c)
            transport = (wx + (0.5 * STEEPEN) * c) * (x_up[k] - x_dn[k])
            transport = transport + wy * (y_up[k] - y_dn[k])
            transport = transport + wz * (z_up - z_dn)
            result.append(c + DIFFUSION * laplace - transport)
        return result

    for a in range(3):
        receive(0, a, pad_a)

    def first_step(x, carry):
        first, last = [None] * (cy // 8), [None] * (cy // 8)
        for y in range(cy):
            new = jnp.concatenate(advance_row(pad_a, x, y), axis=0).astype(BF16).astype(F32)
            pad_b[x + 1, y + 1] = new
            collect_row(first, y, new[:8], 0)
            collect_row(last, y, new[cz - 8 :], 7)
        store_faces(1, x, first, last)
        return carry

    lax.fori_loop(0, cx, first_step, 0)
    for d in range(2):
        out_x[d] = pad_b[1 + (cx - 1) * d, 1 : cy + 1].astype(BF16)
    send(1, 0)
    for d in range(2):
        out_y[d] = pad_b[1 : cx + 1, 1 + (cy - 1) * d].astype(BF16)
    send(1, 1)
    send(1, 2)
    for a in range(3):
        receive(1, a, pad_b)

    gram[...] = jnp.zeros_like(gram)
    ones = jnp.ones((members, half), BF16)

    def second_step(x, pulled):
        for y in range(cy):
            f_out[x, y] = jnp.concatenate(advance_row(pad_b, x, y), axis=0).astype(BF16)
        plane = f_out[x].reshape(cy * cz, members)
        mean = contract(plane, ones, ((1,), (0,))) * (1.0 / members)
        for y in range(cy):
            span = slice(y * cz, (y + 1) * cz)
            level = mean[span]
            root = jnp.broadcast_to(root_w[x, :, y : y + 1], (cz, half))
            pull = pull_v[x, :, y : y + 1] - root * root * level
            both = jnp.concatenate([level, level], axis=1)
            apart = (plane[span].astype(F32) - both).astype(BF16).astype(F32)
            scaled[span] = (apart * jnp.concatenate([root, root], axis=1)).astype(BF16)
            pulled = pulled + apart * jnp.concatenate([pull, pull], axis=1)
        block = scaled[...]
        gram[...] += contract(block, block, ((0,), (0,)))
        return pulled

    pulled = lax.fori_loop(0, cx, second_step, jnp.zeros((cz, members), F32))
    gram_out[:half] = gram[:half, :half]
    gram_out[half : 2 * half] = gram[:half, half:]
    gram_out[2 * half :] = gram[half:, half:]
    total = jnp.sum(pulled, axis=0, keepdims=True)
    coup_out[...] = jnp.concatenate(
        [total[:, :half], total[:, half:], jnp.zeros((6, half), F32)], axis=0
    )

    for step in range(2):
        for a in range(3):
            for d in range(2):
                @pl.when(has[a][d])
                def _():
                    link(step, a, d).wait_send()


def weights_from(tri, coup, half):
    members = 2 * half
    upper = tri[half : 2 * half]
    gram = jnp.concatenate(
        [
            jnp.concatenate([tri[:half], upper], axis=1),
            jnp.concatenate([upper.T, tri[2 * half :]], axis=1),
        ],
        axis=0,
    )
    shape = (members, members)
    diagonal = lax.broadcasted_iota(jnp.int32, shape, 0) == lax.broadcasted_iota(jnp.int32, shape, 1)
    identity = jnp.where(diagonal, 1.0, 0.0).astype(F32)
    coupled = identity + gram
    squares = jnp.sum(jnp.sum(coupled * coupled, axis=0, keepdims=True), axis=1, keepdims=True)
    norm = jnp.sqrt(squares)
    iterate_y = coupled / norm
    iterate_z = None
    for sweep in range(ITERS):
        inner = iterate_y if sweep == 0 else product(iterate_z, iterate_y)
        factor = 1.5 * identity - 0.5 * inner
        iterate_z = factor if sweep == 0 else product(factor, iterate_z)
        if sweep < ITERS - 1:
            iterate_y = product(factor, iterate_y)
    transform = iterate_z / jnp.sqrt(norm)
    coup_row = jnp.concatenate([coup[0:1], coup[1:2]], axis=1)
    coup_col = jnp.sum(jnp.where(diagonal, coup_row, 0.0), axis=1, keepdims=True)
    once_row = jnp.sum(transform * coup_col, axis=0, keepdims=True)
    shift = jnp.sum(transform * once_row, axis=1, keepdims=True)
    return (transform + shift).astype(BF16)


def reduce_kernel(counts, tri, coup, weights_out, outbox, inbox, own, full, semaphores):
    half = tri.shape[1]
    devices = counts[0] * counts[1] * counts[2]
    rows = tri.shape[0] // devices
    pos = [lax.axis_index(a) for a in GRID_AXES]
    rank = (pos[0] * counts[1] + pos[1]) * counts[2] + pos[2]

    def peer(k):
        return lax.rem(rank + k, devices)

    def device(r):
        return {
            "gx": r // (counts[1] * counts[2]),
            "gy": lax.rem(r // counts[2], counts[1]),
            "gz": lax.rem(r, counts[2]),
        }

    barrier = pltpu.get_barrier_semaphore()

    def each(action):
        def body(k, carry):
            action(k)
            return carry

        lax.fori_loop(1, devices, body, 0)

    each(lambda k: pl.semaphore_signal(barrier, inc=1, device_id=device(peer(k)), device_id_type=MESH))
    for i in range(devices):
        outbox[i, :rows] = tri[i * rows : (i + 1) * rows]
        outbox[i, rows:] = coup[...]
    pl.semaphore_wait(barrier, devices - 1)

    def scatter(to, origin):
        return pltpu.make_async_remote_copy(
            src_ref=outbox.at[to],
            dst_ref=inbox.at[origin],
            send_sem=semaphores.at[0, to],
            recv_sem=semaphores.at[1, origin],
            device_id=device(to),
            device_id_type=MESH,
        )

    def gather(to, origin):
        return pltpu.make_async_remote_copy(
            src_ref=own,
            dst_ref=full.at[origin],
            send_sem=semaphores.at[2, to],
            recv_sem=semaphores.at[3, origin],
            device_id=device(to),
            device_id_type=MESH,
        )

    each(lambda k: scatter(peer(k), rank).start())

    def add(k, total):
        scatter(peer(k), peer(k)).wait_recv()
        return total + inbox[peer(k)]

    total = lax.fori_loop(1, devices, add, outbox[rank])
    own[...] = total[:rows]
    full[rank] = total[:rows]
    each(lambda k: gather(peer(k), rank).start())
    each(lambda k: scatter(peer(k), rank).wait_send())
    each(lambda k: gather(peer(k), peer(k)).wait_recv())
    weights_out[...] = weights_from(full[...].reshape(3 * half, half), total[rows:], half)
    each(lambda k: gather(peer(k), rank).wait_send())


def analysis_kernel(f_ref, weights_ref, out_ref):
    shape = f_ref.shape
    members = shape[-1]
    plane = f_ref[...].reshape(-1, members)
    mean = contract(plane, jnp.ones((members, members), BF16), ((1,), (0,))) * (1.0 / members)
    apart = (plane.astype(F32) - mean).astype(BF16)
    mixed = contract(apart, weights_ref[...], ((1,), (0,)))
    out_ref[...] = (mean + mixed).astype(BF16).reshape(shape)


def weights_kernel(tri, coup, weights_out):
    weights_out[...] = weights_from(tri[...], coup[...], tri.shape[1])


def per_device(ensemble, wind_field, obs_value, obs_weight, obs_cell, obs_used):
    cx, cy, cz, members = ensemble.shape
    half = members // 2
    counts = tuple(lax.axis_size(a) for a in GRID_AXES)
    devices = counts[0] * counts[1] * counts[2]
    obs_total = obs_cell.size * devices

    chunked = (-1, 256)
    spot = obs_cell.reshape(chunked)
    spot_xz = spot // (cy * cz) * cz + spot % cz
    spot_y = spot // cz % cy
    strength = obs_used.astype(F32) * obs_weight
    obs_sq = (strength * strength / obs_total).reshape(chunked)
    obs_sv = obs_sq * obs_value.reshape(chunked)
    wind = 0.5 * wind_field.transpose(0, 1, 3, 2)

    forecast, tri, coup = pl.pallas_call(
        functools.partial(forecast_kernel, counts),
        out_shape=(
            jax.ShapeDtypeStruct(ensemble.shape, BF16),
            jax.ShapeDtypeStruct((3 * half, half), F32),
            jax.ShapeDtypeStruct((8, half), F32),
        ),
        in_specs=[VMEM()] * 6,
        out_specs=(VMEM(),) * 3,
        scratch_shapes=[
            pltpu.VMEM((cx + 2, cy + 2, cz, members), F32),
            pltpu.VMEM((cx + 2, cy + 2, cz, members), F32),
            pltpu.VMEM((2, cx, cy, members), F32),
            pltpu.VMEM((2, 2, cy, cz, members), BF16),
            pltpu.VMEM((2, 2, cx, cz, members), BF16),
            pltpu.VMEM((2, 2, cx, cy, members), BF16),
            pltpu.VMEM((2, cy, cz, members), BF16),
            pltpu.VMEM((2, cx, cz, members), BF16),
            pltpu.VMEM((2, 2, cx, cy, members), BF16),
            pltpu.VMEM((cx * cz, 6 * cy), F32),
            pltpu.VMEM((cx, cz, cy), F32),
            pltpu.VMEM((cx, cz, cy), F32),
            pltpu.VMEM((cy * cz, members), BF16),
            pltpu.VMEM((members, members), F32),
            pltpu.SemaphoreType.DMA((2, 3, 2)),
            pltpu.SemaphoreType.DMA((2, 3, 2)),
        ],
        compiler_params=pltpu.CompilerParams(
            collective_id=0, has_side_effects=True, vmem_limit_bytes=VMEM_LIMIT
        ),
    )(ensemble, wind, spot_xz, spot_y, obs_sq, obs_sv)

    weights_shape = jax.ShapeDtypeStruct((members, members), BF16)
    if devices > 1 and (3 * half // 8) % devices == 0:
        rows = 3 * half // devices
        weights = pl.pallas_call(
            functools.partial(reduce_kernel, counts),
            out_shape=weights_shape,
            in_specs=[VMEM()] * 2,
            out_specs=VMEM(),
            scratch_shapes=[
                pltpu.VMEM((devices, rows + 8, half), F32),
                pltpu.VMEM((devices, rows + 8, half), F32),
                pltpu.VMEM((rows, half), F32),
                pltpu.VMEM((devices, rows, half), F32),
                pltpu.SemaphoreType.DMA((4, devices)),
            ],
            compiler_params=pltpu.CompilerParams(
                collective_id=1, has_side_effects=True, vmem_limit_bytes=VMEM_LIMIT
            ),
        )(tri, coup)
    else:
        tri, coup = lax.psum((tri, coup), GRID_AXES)
        weights = pl.pallas_call(
            weights_kernel,
            out_shape=weights_shape,
            in_specs=[VMEM()] * 2,
            out_specs=VMEM(),
            compiler_params=pltpu.CompilerParams(vmem_limit_bytes=VMEM_LIMIT),
        )(tri, coup)

    planes = 4
    block = pl.BlockSpec((planes, cy, cz, members), lambda i: (i, 0, 0, 0))
    return pl.pallas_call(
        analysis_kernel,
        grid=(cx // planes,),
        out_shape=jax.ShapeDtypeStruct(ensemble.shape, BF16),
        in_specs=[block, pl.BlockSpec((members, members), lambda i: (0, 0))],
        out_specs=block,
        compiler_params=pltpu.CompilerParams(vmem_limit_bytes=VMEM_LIMIT),
    )(forecast, weights)


def solution(mesh):
    cells = P(("grp", "gx"), "gy", "gz")
    in_specs = (
        P(("grp", "gx"), "gy", "gz", None),
        P(None, ("grp", "gx"), "gy", "gz"),
        cells,
        cells,
        cells,
        cells,
    )
    out_specs = P(("grp", "gx"), "gy", "gz", None)
    return jax.shard_map(
        per_device, mesh=mesh, in_specs=in_specs, out_specs=out_specs, check_vma=False
    )
```

time: 222 us -> 63.7 us (0.29)
  waiting for transfers between devices: 65.8 us -> 0 us
  Pallas kernels: 0 us -> 56.8 us
  blocking collectives: 36.1 us -> 0 us
  starting transfers between devices: 32.6 us -> 0 us
  other arithmetic: 31.8 us -> 2.9 us
  local copies, waits for them, and re-layouts: 29.1 us -> 3.44 us
  between operations: 14.7 us -> 0.08 us
  matrix products: 11.2 us -> 0 us
    pallas_call x0 -> x3, Pallas kernels: none -> 56.8 us  [the longest x1 29.5 us: per_device(): pl.pallas_call(functools.partial(forecast_kernel, counts), out_shape=(jax...]
    psum x1 -> x0, waiting for transfers between devices: 55.9 us -> none  [per_device(): gram_full, coupling = lax.psum((gram_part, couple_part), ('gx', 'gy', 'gz'))]
    psum x1 -> x0, blocking collectives: 36.1 us -> none  [per_device(): gram_full, coupling = lax.psum((gram_part, couple_part), ('gx', 'gy', 'gz'))]
    ppermute x12 -> x0, starting transfers between devices: 32.6 us -> none  [the longest x6 24.8 us: padded_2(): lax.ppermute(lax.slice_in_dim(block, block.shape[dim] - width, None, axis...]
    convert_element_type x5 -> x0, other arithmetic: 27.3 us -> none  [the longest x2 23.6 us: advance(): (centre + diffusion * laplace - 0.5 * transport).astype(jnp.bfloat16)]
    gather x2 -> x0, local copies, waits for them, and re-layouts: 20.8 us -> none  [the longest x1 11.8 us: per_device(): mean_at = jnp.take(mean_flat, obs_spots, axis=0)]
    dot_general x19 -> x0, matrix products: 11.2 us -> none  [the longest x16 7.69 us: product(): return jnp.dot(left, right, precision=lax.Precision.HIGHEST)]
    ppermute x12 -> x0, waiting for transfers between devices: 9.97 us -> none  [the longest x6 5.37 us: padded_2(): lax.ppermute(lax.slice_in_dim(block, block.shape[dim] - width, None, axis...]
  transfers between devices with their start and end apart: 13 -> 0, of which waited for: 9 -> 0; matrix products, arithmetic and copies ran while one was open for 3% -> 0% of each run, Pallas kernels for 0% -> 0%
where the time goes in v1:
time: 63.7 us; the launch traced here: 63.3 us
  Pallas kernels  56.8 us (89%)
  local copies, waits for them, and re-layouts  3.44 us (5%)
  other arithmetic  2.9 us (5%)
    pallas_call x1, Pallas kernels, per_device(): pl.pallas_call(functools.partial(forecast_kernel, counts), out_shape=(jax...  29.5 us
    pallas_call x1, Pallas kernels, per_device(): pl.pallas_call(functools.partial(reduce_kernel, counts), out_shape=weight...  22.5 us
    pallas_call x1, Pallas kernels, per_device(): pl.pallas_call(analysis_kernel, grid=(cx // planes,), out_shape=jax.Shape...  4.83 us
    unnamed x5, local copies, waits for them, and re-layouts  3.01 us

profile of v1, /device:TPU:0, one launch (start us, length us, event | category | flops | bytes accessed | tf_op | source)
XLA Modules:
  0.0 63.3 jit_solution(11440950216900969809)
XLA Ops:
  0.0 0.9 %multiply_multiply_fusion = f32[16,16,8]{1,2,0:T(8,128)S(1)} fusion(f32[16,16,8]{1,2,0:T(8,128)} %param.9, s32[16,16,8]{1,2,0:T(8,128)} %param.11), kind=kLoop, calls=%fused_computation.1 | loop fusion | flops 8192 | bytes 24576 | tf_op jit(solution)/shard_map/div | solution.py:364
  0.9 0.1 copy.13
  1.0 0.1 reshape.10.obs_sq
  1.1 0.0 copy-start
  1.1 0.9 %copy.14 = f32[16,16,8]{2,1,0:T(8,128)S(1)} copy(f32[16,16,8]{1,2,0:T(8,128)} %param.8) | data formatting | bytes 16384 | tf_op args[2]
  2.0 0.1 reshape.11
  2.2 0.6 mul.30.obs_sv
  2.8 0.9 %copy.12 = s32[16,16,8]{2,1,0:T(8,128)S(1)} copy(s32[16,16,8]{1,2,0:T(8,128)} %param.10) | data formatting | bytes 16384 | tf_op args[4]
  3.7 0.1 reshape.9
  3.8 0.6 add_select_fusion
  4.5 1.2 %copy.11 = f32[3,16,16,16]{2,3,1,0:T(8,128)S(1)} copy(f32[3,16,16,16]{3,2,1,0:T(8,128)} %param.7) | data formatting | bytes 98304 | tf_op args[1]
  5.6 0.8 %multiply_bitcast_fusion.wind = f32[3,16,16,16]{3,2,1,0:T(8,128)} fusion(f32[3,16,16,16]{2,3,1,0:T(8,128)S(1)} %copy.11), kind=kLoop, calls=%fused_computation | loop fusion | flops 12288 | bytes 98304 | tf_op jit(solution)/shard_map/mul | solution.py:366
  6.4 0.0 copy-done
  6.4 29.5 %shard_map.64 = (bf16[16,16,16,256]{3,2,1,0:T(8,128)(2,1)}, f32[384,128]{1,0:T(8,128)}, f32[8,128]{1,0:T(8,128)}) custom-call(bf16[16,16,16,256]{3,2,1,0:T(8,128)(2,1)} %ens.1, f32[3,16,16,16]{3,2,1,0:T(8,128)} %multiply_bitcast_fusion.wind, s32[8,256]{1,0:T(8,128)} %get-tuple-element.12.spot_xz, s32[8,256]{1,0:T(8,128)} %get-tuple-element.11.spot_y, ...), custom_call_target="tpu_custom_call" | custom-call | tf_op jit(solution)/shard_map/pallas_call | solution.py:368
  35.9 22.5 %shard_map.65.weights_ref = bf16[256,256]{1,0:T(8,128)(2,1)} custom-call(f32[384,128]{1,0:T(8,128)} %get-tuple-element.9.tri, f32[8,128]{1,0:T(8,128)} %get-tuple-element.10.coup), custom_call_target="tpu_custom_call" | custom-call | tf_op jit(solution)/shard_map/pallas_call | solution.py:403
  58.4 4.8 %shard_map.66 = bf16[16,16,16,256]{3,2,1,0:T(8,128)(2,1)} custom-call(bf16[16,16,16,256]{3,2,1,0:T(8,128)(2,1)} %get-tuple-element.8.f_ref, bf16[256,256]{1,0:T(8,128)(2,1)} %shard_map.65.weights_ref), custom_call_target="tpu_custom_call" | custom-call | tf_op jit(solution)/shard_map/pallas_call | solution.py:431
Async XLA Ops:
  1.1 5.3 %copy-start = (f32[8,256]{1,0:T(8,128)}, f32[8,256]{1,0:T(8,128)S(1)}, u32[]{:S(2)}) copy-start(f32[8,256]{1,0:T(8,128)S(1)} %reshape.10.obs_sq) | copy-start | bytes 24580

commit v2 on v1

--- a/solution.py
+++ b/solution.py
@@ -18,8 +18,17 @@
 VMEM_LIMIT = 56 * 1024 * 1024
 
 
-def product(left, right):
-    return jnp.dot(left, right, precision=lax.Precision.HIGHEST, preferred_element_type=F32)
+def halves(value):
+    high = value.astype(BF16)
+    return high, (value - high.astype(F32)).astype(BF16)
+
+
+def product(left, *rights):
+    high, low = halves(left)
+    wide = jnp.concatenate([high, high, low], axis=1)
+    parts = [halves(right) for right in rights]
+    tall = [jnp.concatenate([high, low, high], axis=0) for high, low in parts]
+    return contract(wide, jnp.concatenate(tall, axis=1), ((1,), (0,)))
 
 
 def contract(left, right, dims):
@@ -33,13 +42,14 @@
     faces[y // 8] = moved if faces[y // 8] is None else jnp.where(rows == y % 8, moved, faces[y // 8])
 
 
-def forecast_kernel(
-    counts, ens, wind, spot_xz, spot_y, obs_sq, obs_sv,
+def forecast_body(
+    counts, enter, ens, wind, obs_value, obs_weight, obs_cell, obs_used,
     f_out, gram_out, coup_out,
-    pad_a, pad_b, halo_z, in_x, in_y, in_z, out_x, out_y, out_z,
-    obs_acc, root_w, pull_v, scaled, gram, send_sem, recv_sem,
+    pad_a, pad_b, halo_z, in_x, in_y, in_z, out_x, out_y, out_z, wind_t,
+    spot_xz, spot_y, obs_sq, obs_sv, obs_acc, root_w, pull_v, scaled, gram, send_sem, recv_sem,
 ):
     cx, cy, cz, members = ens.shape
+    obs_total = obs_cell.size * counts[0] * counts[1] * counts[2]
     half = members // 2
     pos = [lax.axis_index(a) for a in GRID_AXES]
     has = [(pos[a] > 0, pos[a] < counts[a] - 1) for a in range(3)]
@@ -90,15 +100,7 @@
             def _():
                 border(jnp.zeros(inbox[a].shape[2:], F32))
 
-    barrier = pltpu.get_barrier_semaphore()
-    for a in range(3):
-        for d in range(2):
-            @pl.when(has[a][d])
-            def _():
-                pl.semaphore_signal(barrier, inc=1, device_id=target(a, d), device_id_type=MESH)
-    neighbours = sum(has[a][d].astype(jnp.int32) for a in range(3) for d in range(2))
-    pl.semaphore_wait(barrier, neighbours)
-
+    enter(has, target)
     send(0, 0)
     send(0, 1)
 
@@ -114,6 +116,8 @@
             collect_row(first, y, v[:8], 0)
             collect_row(last, y, v[cz - 8 :], 7)
         store_faces(0, x, first, last)
+        for i in range(3):
+            wind_t[i, x] = 0.5 * wind[i, x].T
         return carry
 
     lax.fori_loop(0, cx, widen, 0)
@@ -121,6 +125,17 @@
 
     obs_acc[...] = jnp.zeros_like(obs_acc)
     chunks, chunk = spot_xz.shape
+
+    def turned(ref):
+        return ref[...].reshape(chunk, chunks).T
+
+    cell = turned(obs_cell)
+    spot_xz[...] = cell // (cy * cz) * cz + cell % cz
+    spot_y[...] = cell // cz % cy
+    strength = turned(obs_used).astype(F32) * turned(obs_weight)
+    squared = strength * strength * (1.0 / obs_total)
+    obs_sq[...] = squared
+    obs_sv[...] = squared * turned(obs_value)
 
     def scatter(i, carry):
         row = pl.ds(i, 1)
@@ -165,7 +180,7 @@
             c = centre[k]
             z_up = jnp.where(bottom, rolled_up[k + 1], rolled_up[k])
             z_dn = jnp.where(top, rolled_dn[k], rolled_dn[k + 1])
-            wx, wy, wz = (wind[i, x, 8 * k : 8 * k + 8, y : y + 1] for i in range(3))
+            wx, wy, wz = (wind_t[i, x, 8 * k : 8 * k + 8, y : y + 1] for i in range(3))
             laplace = ((x_up[k] + x_dn[k]) + (y_up[k] + y_dn[k])) + ((z_up + z_dn) - 6.0 * c)
             transport = (wx + (0.5 * STEEPEN) * c) * (x_up[k] - x_dn[k])
             transport = transport + wy * (y_up[k] - y_dn[k])
@@ -227,12 +242,30 @@
         [total[:, :half], total[:, half:], jnp.zeros((6, half), F32)], axis=0
     )
 
-    for step in range(2):
-        for a in range(3):
-            for d in range(2):
-                @pl.when(has[a][d])
-                def _():
-                    link(step, a, d).wait_send()
+    def finish():
+        for step in range(2):
+            for a in range(3):
+                for d in range(2):
+                    @pl.when(has[a][d])
+                    def _():
+                        link(step, a, d).wait_send()
+
+    return finish
+
+
+def enter_beside(has, target):
+    barrier = pltpu.get_barrier_semaphore()
+    for a in range(3):
+        for d in range(2):
+            @pl.when(has[a][d])
+            def _():
+                pl.semaphore_signal(barrier, inc=1, device_id=target(a, d), device_id_type=MESH)
+    neighbours = sum(has[a][d].astype(jnp.int32) for a in range(3) for d in range(2))
+    pl.semaphore_wait(barrier, neighbours)
+
+
+def forecast_kernel(counts, *refs):
+    forecast_body(counts, enter_beside, *refs)()
 
 
 def weights_from(tri, coup, half):
@@ -256,18 +289,26 @@
     for sweep in range(ITERS):
         inner = iterate_y if sweep == 0 else product(iterate_z, iterate_y)
         factor = 1.5 * identity - 0.5 * inner
-        iterate_z = factor if sweep == 0 else product(factor, iterate_z)
-        if sweep < ITERS - 1:
-            iterate_y = product(factor, iterate_y)
+        if sweep == 0:
+            iterate_y, iterate_z = product(factor, iterate_y), factor
+        elif sweep < ITERS - 1:
+            both = product(factor, iterate_y, iterate_z)
+            iterate_y, iterate_z = both[:, :members], both[:, members:]
+        else:
+            iterate_z = product(factor, iterate_z)
     transform = iterate_z / jnp.sqrt(norm)
     coup_row = jnp.concatenate([coup[0:1], coup[1:2]], axis=1)
     coup_col = jnp.sum(jnp.where(diagonal, coup_row, 0.0), axis=1, keepdims=True)
     once_row = jnp.sum(transform * coup_col, axis=0, keepdims=True)
     shift = jnp.sum(transform * once_row, axis=1, keepdims=True)
-    return (transform + shift).astype(BF16)
-
-
-def reduce_kernel(counts, tri, coup, weights_out, outbox, inbox, own, full, semaphores):
+    weights = (transform + shift).astype(BF16).astype(F32)
+    folded = weights + (1.0 - jnp.sum(weights, axis=0, keepdims=True)) / members
+    return jnp.concatenate(halves(folded), axis=0)
+
+
+def whole_kernel(counts, *refs):
+    inputs, f_hbm, weights_out = refs[:6], refs[6], refs[7]
+    outbox, inbox, own, full, semaphores, f_vmem, tri, coup, f_sem = refs[8:17]
     half = tri.shape[1]
     devices = counts[0] * counts[1] * counts[2]
     rows = tri.shape[0] // devices
@@ -284,8 +325,6 @@
             "gz": lax.rem(r, counts[2]),
         }
 
-    barrier = pltpu.get_barrier_semaphore()
-
     def each(action):
         def body(k, carry):
             action(k)
@@ -293,11 +332,21 @@
 
         lax.fori_loop(1, devices, body, 0)
 
-    each(lambda k: pl.semaphore_signal(barrier, inc=1, device_id=device(peer(k)), device_id_type=MESH))
+    def enter(has, target):
+        barrier = pltpu.get_barrier_semaphore()
+        each(
+            lambda k: pl.semaphore_signal(
+                barrier, inc=1, device_id=device(peer(k)), device_id_type=MESH
+            )
+        )
+        pl.semaphore_wait(barrier, devices - 1)
+
+    finish = forecast_body(counts, enter, *inputs, f_vmem, tri, coup, *refs[17:])
+    write = pltpu.make_async_copy(f_vmem, f_hbm, f_sem)
+    write.start()
     for i in range(devices):
         outbox[i, :rows] = tri[i * rows : (i + 1) * rows]
         outbox[i, rows:] = coup[...]
-    pl.semaphore_wait(barrier, devices - 1)
 
     def scatter(to, origin):
         return pltpu.make_async_remote_copy(
@@ -333,16 +382,16 @@
     each(lambda k: gather(peer(k), peer(k)).wait_recv())
     weights_out[...] = weights_from(full[...].reshape(3 * half, half), total[rows:], half)
     each(lambda k: gather(peer(k), rank).wait_send())
-
-
-def analysis_kernel(f_ref, weights_ref, out_ref):
+    finish()
+    write.wait()
+
+
+def analysis_kernel(f_ref, folded_ref, out_ref):
     shape = f_ref.shape
     members = shape[-1]
     plane = f_ref[...].reshape(-1, members)
-    mean = contract(plane, jnp.ones((members, members), BF16), ((1,), (0,))) * (1.0 / members)
-    apart = (plane.astype(F32) - mean).astype(BF16)
-    mixed = contract(apart, weights_ref[...], ((1,), (0,)))
-    out_ref[...] = (mean + mixed).astype(BF16).reshape(shape)
+    twice = jnp.concatenate([plane, plane], axis=1)
+    out_ref[...] = contract(twice, folded_ref[...], ((1,), (0,))).astype(BF16).reshape(shape)
 
 
 def weights_kernel(tri, coup, weights_out):
@@ -354,73 +403,76 @@
     half = members // 2
     counts = tuple(lax.axis_size(a) for a in GRID_AXES)
     devices = counts[0] * counts[1] * counts[2]
-    obs_total = obs_cell.size * devices
-
-    chunked = (-1, 256)
-    spot = obs_cell.reshape(chunked)
-    spot_xz = spot // (cy * cz) * cz + spot % cz
-    spot_y = spot // cz % cy
-    strength = obs_used.astype(F32) * obs_weight
-    obs_sq = (strength * strength / obs_total).reshape(chunked)
-    obs_sv = obs_sq * obs_value.reshape(chunked)
-    wind = 0.5 * wind_field.transpose(0, 1, 3, 2)
-
-    forecast, tri, coup = pl.pallas_call(
-        functools.partial(forecast_kernel, counts),
-        out_shape=(
-            jax.ShapeDtypeStruct(ensemble.shape, BF16),
-            jax.ShapeDtypeStruct((3 * half, half), F32),
-            jax.ShapeDtypeStruct((8, half), F32),
-        ),
-        in_specs=[VMEM()] * 6,
-        out_specs=(VMEM(),) * 3,
-        scratch_shapes=[
-            pltpu.VMEM((cx + 2, cy + 2, cz, members), F32),
-            pltpu.VMEM((cx + 2, cy + 2, cz, members), F32),
-            pltpu.VMEM((2, cx, cy, members), F32),
-            pltpu.VMEM((2, 2, cy, cz, members), BF16),
-            pltpu.VMEM((2, 2, cx, cz, members), BF16),
-            pltpu.VMEM((2, 2, cx, cy, members), BF16),
-            pltpu.VMEM((2, cy, cz, members), BF16),
-            pltpu.VMEM((2, cx, cz, members), BF16),
-            pltpu.VMEM((2, 2, cx, cy, members), BF16),
-            pltpu.VMEM((cx * cz, 6 * cy), F32),
-            pltpu.VMEM((cx, cz, cy), F32),
-            pltpu.VMEM((cx, cz, cy), F32),
-            pltpu.VMEM((cy * cz, members), BF16),
-            pltpu.VMEM((members, members), F32),
-            pltpu.SemaphoreType.DMA((2, 3, 2)),
-            pltpu.SemaphoreType.DMA((2, 3, 2)),
-        ],
-        compiler_params=pltpu.CompilerParams(
-            collective_id=0, has_side_effects=True, vmem_limit_bytes=VMEM_LIMIT
-        ),
-    )(ensemble, wind, spot_xz, spot_y, obs_sq, obs_sv)
-
-    weights_shape = jax.ShapeDtypeStruct((members, members), BF16)
+    chunk, chunks = cx * cy, obs_cell.shape[2]
+    arguments = (ensemble, wind_field, obs_value, obs_weight, obs_cell, obs_used)
+    forecast_shape = jax.ShapeDtypeStruct(ensemble.shape, BF16)
+    folded_shape = jax.ShapeDtypeStruct((2 * members, members), BF16)
+    tri_shape, coup_shape = (3 * half, half), (8, half)
+    forecast_scratch = [
+        pltpu.VMEM((cx + 2, cy + 2, cz, members), F32),
+        pltpu.VMEM((cx + 2, cy + 2, cz, members), F32),
+        pltpu.VMEM((2, cx, cy, members), F32),
+        pltpu.VMEM((2, 2, cy, cz, members), BF16),
+        pltpu.VMEM((2, 2, cx, cz, members), BF16),
+        pltpu.VMEM((2, 2, cx, cy, members), BF16),
+        pltpu.VMEM((2, cy, cz, members), BF16),
+        pltpu.VMEM((2, cx, cz, members), BF16),
+        pltpu.VMEM((2, 2, cx, cy, members), BF16),
+        pltpu.VMEM((3, cx, cz, cy), F32),
+        pltpu.VMEM((chunks, chunk), jnp.int32),
+        pltpu.VMEM((chunks, chunk), jnp.int32),
+        pltpu.VMEM((chunks, chunk), F32),
+        pltpu.VMEM((chunks, chunk), F32),
+        pltpu.VMEM((cx * cz, 6 * cy), F32),
+        pltpu.VMEM((cx, cz, cy), F32),
+        pltpu.VMEM((cx, cz, cy), F32),
+        pltpu.VMEM((cy * cz, members), BF16),
+        pltpu.VMEM((members, members), F32),
+        pltpu.SemaphoreType.DMA((2, 3, 2)),
+        pltpu.SemaphoreType.DMA((2, 3, 2)),
+    ]
     if devices > 1 and (3 * half // 8) % devices == 0:
         rows = 3 * half // devices
-        weights = pl.pallas_call(
-            functools.partial(reduce_kernel, counts),
-            out_shape=weights_shape,
-            in_specs=[VMEM()] * 2,
-            out_specs=VMEM(),
+        forecast, folded = pl.pallas_call(
+            functools.partial(whole_kernel, counts),
+            out_shape=(forecast_shape, folded_shape),
+            in_specs=[VMEM()] * 6,
+            out_specs=(pl.BlockSpec(memory_space=pl.ANY), VMEM()),
             scratch_shapes=[
                 pltpu.VMEM((devices, rows + 8, half), F32),
                 pltpu.VMEM((devices, rows + 8, half), F32),
                 pltpu.VMEM((rows, half), F32),
                 pltpu.VMEM((devices, rows, half), F32),
                 pltpu.SemaphoreType.DMA((4, devices)),
-            ],
+                pltpu.VMEM(ensemble.shape, BF16),
+                pltpu.VMEM(tri_shape, F32),
+                pltpu.VMEM(coup_shape, F32),
+                pltpu.SemaphoreType.DMA,
+            ]
+            + forecast_scratch,
             compiler_params=pltpu.CompilerParams(
-                collective_id=1, has_side_effects=True, vmem_limit_bytes=VMEM_LIMIT
+                collective_id=0, has_side_effects=True, vmem_limit_bytes=VMEM_LIMIT
             ),
-        )(tri, coup)
+        )(*arguments)
     else:
+        forecast, tri, coup = pl.pallas_call(
+            functools.partial(forecast_kernel, counts),
+            out_shape=(
+                forecast_shape,
+                jax.ShapeDtypeStruct(tri_shape, F32),
+                jax.ShapeDtypeStruct(coup_shape, F32),
+            ),
+            in_specs=[VMEM()] * 6,
+            out_specs=(VMEM(),) * 3,
+            scratch_shapes=forecast_scratch,
+            compiler_params=pltpu.CompilerParams(
+                collective_id=0, has_side_effects=True, vmem_limit_bytes=VMEM_LIMIT
+            ),
+        )(*arguments)
         tri, coup = lax.psum((tri, coup), GRID_AXES)
-        weights = pl.pallas_call(
+        folded = pl.pallas_call(
             weights_kernel,
-            out_shape=weights_shape,
+            out_shape=folded_shape,
             in_specs=[VMEM()] * 2,
             out_specs=VMEM(),
             compiler_params=pltpu.CompilerParams(vmem_limit_bytes=VMEM_LIMIT),
@@ -432,10 +484,10 @@
         analysis_kernel,
         grid=(cx // planes,),
         out_shape=jax.ShapeDtypeStruct(ensemble.shape, BF16),
-        in_specs=[block, pl.BlockSpec((members, members), lambda i: (0, 0))],
+        in_specs=[block, pl.BlockSpec((2 * members, members), lambda i: (0, 0))],
         out_specs=block,
         compiler_params=pltpu.CompilerParams(vmem_limit_bytes=VMEM_LIMIT),
-    )(forecast, weights)
+    )(forecast, folded)
 
 
 def solution(mesh):

time: 63.7 us -> 58.8 us (0.923)
  Pallas kernels: 56.8 us -> 52 us
  local copies, waits for them, and re-layouts: 3.44 us -> 6.37 us
  other arithmetic: 2.9 us -> 0 us
    pallas_call x2 -> x1, Pallas kernels: 52 us -> 47.3 us  [per_device(): pl.pallas_call(functools.partial(whole_kernel, counts), out_shape=(foreca...]
    unnamed x5 -> x4, local copies, waits for them, and re-layouts: 3.01 us -> 6.37 us
    mul x2 -> x0, other arithmetic: 1.39 us -> none  [the longest x1 0.78 us: per_device(): wind = 0.5 * wind_field.transpose(0, 1, 3, 2)]
    div x1 -> x0, other arithmetic: 0.88 us -> none  [per_device(): obs_sq = (strength * strength / obs_total).reshape(chunked)]
where the time goes in v2:
time: 58.8 us; the launch traced here: 58.4 us
  Pallas kernels  52 us (88%)
  local copies, waits for them, and re-layouts  6.37 us (11%)
    pallas_call x1, Pallas kernels, per_device(): pl.pallas_call(functools.partial(whole_kernel, counts), out_shape=(foreca...  47.3 us
    unnamed x4, local copies, waits for them, and re-layouts  6.37 us
    pallas_call x1, Pallas kernels, per_device(): pl.pallas_call(analysis_kernel, grid=(cx // planes,), out_shape=jax.Shape...  4.66 us

profile of v2, /device:TPU:0, one launch (start us, length us, event | category | flops | bytes accessed | tf_op | source)
XLA Modules:
  0.0 58.4 jit_solution(3927179439532346345)
XLA Ops:
  0.0 1.6 %copy.7.refs_2_ = f32[16,16,8]{2,1,0:T(8,128)} copy(f32[16,16,8]{1,2,0:T(8,128)} %param.8) | data formatting | bytes 16384 | tf_op args[2]
  1.6 1.6 %copy.8.refs_3_ = f32[16,16,8]{2,1,0:T(8,128)} copy(f32[16,16,8]{1,2,0:T(8,128)} %param.9) | data formatting | bytes 16384 | tf_op args[3]
  3.2 1.6 %copy.9.refs_4_ = s32[16,16,8]{2,1,0:T(8,128)} copy(s32[16,16,8]{1,2,0:T(8,128)} %param.10) | data formatting | bytes 16384 | tf_op args[4]
  4.8 1.6 %copy.10.refs_5_ = s32[16,16,8]{2,1,0:T(8,128)} copy(s32[16,16,8]{1,2,0:T(8,128)} %param.11) | data formatting | bytes 16384 | tf_op args[5]
  6.4 47.3 %shard_map.64 = (bf16[16,16,16,256]{3,2,1,0:T(8,128)(2,1)}, bf16[512,256]{1,0:T(8,128)(2,1)}) custom-call(bf16[16,16,16,256]{3,2,1,0:T(8,128)(2,1)} %refs_0_.1, f32[3,16,16,16]{3,2,1,0:T(8,128)} %refs_1_.1, f32[16,16,8]{2,1,0:T(8,128)} %copy.7.refs_2_, f32[16,16,8]{2,1,0:T(8,128)} %copy.8.refs_3_, s32[16,16,8]{2,1,0:T(8,128)} %copy.9.refs_4_, ...), custom_call_target="tpu_custom_call" | custom-call | tf_op jit(solution)/shard_map/pallas_call | solution.py:436
  53.7 4.7 %shard_map.65 = bf16[16,16,16,256]{3,2,1,0:T(8,128)(2,1)} custom-call(bf16[16,16,16,256]{3,2,1,0:T(8,128)(2,1)} %get-tuple-element.7.f_ref, bf16[512,256]{1,0:T(8,128)(2,1)} %get-tuple-element.8.folded_ref), custom_call_target="tpu_custom_call" | custom-call | tf_op jit(solution)/shard_map/pallas_call | solution.py:483

commit v3 on v2

--- a/solution.py
+++ b/solution.py
@@ -403,8 +403,9 @@
     half = members // 2
     counts = tuple(lax.axis_size(a) for a in GRID_AXES)
     devices = counts[0] * counts[1] * counts[2]
-    chunk, chunks = cx * cy, obs_cell.shape[2]
-    arguments = (ensemble, wind_field, obs_value, obs_weight, obs_cell, obs_used)
+    chunk, chunks = cx * obs_cell.shape[2], cy
+    observed = (obs_value, obs_weight, obs_cell, obs_used)
+    arguments = (ensemble, wind_field) + tuple(v.transpose(0, 2, 1) for v in observed)
     forecast_shape = jax.ShapeDtypeStruct(ensemble.shape, BF16)
     folded_shape = jax.ShapeDtypeStruct((2 * members, members), BF16)
     tri_shape, coup_shape = (3 * half, half), (8, half)

time: 58.8 us -> 52.9 us (0.90)
  local copies, waits for them, and re-layouts: 6.37 us -> 0 us
  Pallas kernels: 52 us -> 52.7 us
    unnamed x4 -> x0, local copies, waits for them, and re-layouts: 6.37 us -> none
    pallas_call x1, Pallas kernels: 47.3 us -> 48 us  [per_device(): pl.pallas_call(functools.partial(whole_kernel, counts), out_shape=(foreca...]
where the time goes in v3:
time: 52.9 us; the launch traced here: 52.7 us
  Pallas kernels  52.7 us (100%)
    pallas_call x1, Pallas kernels, per_device(): pl.pallas_call(functools.partial(whole_kernel, counts), out_shape=(foreca...  48 us
    pallas_call x1, Pallas kernels, per_device(): pl.pallas_call(analysis_kernel, grid=(cx // planes,), out_shape=jax.Shape...  4.66 us

profile of v3, /device:TPU:0, one launch (start us, length us, event | category | flops | bytes accessed | tf_op | source)
XLA Modules:
  0.0 52.7 jit_solution(8601192978859190600)
XLA Ops:
  0.0 48.0 %shard_map.64 = (bf16[16,16,16,256]{3,2,1,0:T(8,128)(2,1)}, bf16[512,256]{1,0:T(8,128)(2,1)}) custom-call(bf16[16,16,16,256]{3,2,1,0:T(8,128)(2,1)} %refs_0_.1, f32[3,16,16,16]{3,2,1,0:T(8,128)} %refs_1_.1, f32[16,8,16]{2,1,0:T(8,128)} %bitcast.4, f32[16,8,16]{2,1,0:T(8,128)} %bitcast.5, s32[16,8,16]{2,1,0:T(8,128)} %bitcast.6, s32[16,8,16]{2,1,0:T(8,128)} %bitcast.7), custom_call_target="tpu_custom_call" | custom-call | tf_op jit(solution)/shard_map/pallas_call | solution.py:437
  48.0 4.7 %shard_map.65 = bf16[16,16,16,256]{3,2,1,0:T(8,128)(2,1)} custom-call(bf16[16,16,16,256]{3,2,1,0:T(8,128)(2,1)} %get-tuple-element.7.f_ref, bf16[512,256]{1,0:T(8,128)(2,1)} %get-tuple-element.8.folded_ref), custom_call_target="tpu_custom_call" | custom-call | tf_op jit(solution)/shard_map/pallas_call | solution.py:484

commit v4 on v3

--- a/solution.py
+++ b/solution.py
@@ -201,10 +201,11 @@
         store_faces(1, x, first, last)
         return carry
 
-    lax.fori_loop(0, cx, first_step, 0)
+    lax.fori_loop(0, 2, lambda i, carry: first_step(i * (cx - 1), carry), 0)
     for d in range(2):
         out_x[d] = pad_b[1 + (cx - 1) * d, 1 : cy + 1].astype(BF16)
     send(1, 0)
+    lax.fori_loop(1, cx - 1, first_step, 0)
     for d in range(2):
         out_y[d] = pad_b[1 : cx + 1, 1 + (cy - 1) * d].astype(BF16)
     send(1, 1)
@@ -479,7 +480,7 @@
             compiler_params=pltpu.CompilerParams(vmem_limit_bytes=VMEM_LIMIT),
         )(tri, coup)
 
-    planes = 4
+    planes = 8
     block = pl.BlockSpec((planes, cy, cz, members), lambda i: (i, 0, 0, 0))
     return pl.pallas_call(
         analysis_kernel,

time: 52.9 us -> 51 us (0.964)
  Pallas kernels: 52.7 us -> 50.8 us
    pallas_call x1, Pallas kernels: 4.66 us -> 3.68 us  [per_device(): pl.pallas_call(analysis_kernel, grid=(cx // planes,), out_shape=jax.Shape...]
    pallas_call x1, Pallas kernels: 48 us -> 47.1 us  [per_device(): pl.pallas_call(functools.partial(whole_kernel, counts), out_shape=(foreca...]
where the time goes in v4:
time: 51 us; the launch traced here: 50.8 us
  Pallas kernels  50.8 us (100%)
    pallas_call x1, Pallas kernels, per_device(): pl.pallas_call(functools.partial(whole_kernel, counts), out_shape=(foreca...  47.1 us
    pallas_call x1, Pallas kernels, per_device(): pl.pallas_call(analysis_kernel, grid=(cx // planes,), out_shape=jax.Shape...  3.68 us

profile of v4, /device:TPU:0, one launch (start us, length us, event | category | flops | bytes accessed | tf_op | source)
XLA Modules:
  0.0 50.8 jit_solution(5212546334680678618)
XLA Ops:
  0.0 47.1 %shard_map.64 = (bf16[16,16,16,256]{3,2,1,0:T(8,128)(2,1)}, bf16[512,256]{1,0:T(8,128)(2,1)}) custom-call(bf16[16,16,16,256]{3,2,1,0:T(8,128)(2,1)} %refs_0_.1, f32[3,16,16,16]{3,2,1,0:T(8,128)} %refs_1_.1, f32[16,8,16]{2,1,0:T(8,128)} %bitcast.4, f32[16,8,16]{2,1,0:T(8,128)} %bitcast.5, s32[16,8,16]{2,1,0:T(8,128)} %bitcast.6, s32[16,8,16]{2,1,0:T(8,128)} %bitcast.7), custom_call_target="tpu_custom_call" | custom-call | tf_op jit(solution)/shard_map/pallas_call | solution.py:438
  47.1 3.7 %shard_map.65 = bf16[16,16,16,256]{3,2,1,0:T(8,128)(2,1)} custom-call(bf16[16,16,16,256]{3,2,1,0:T(8,128)(2,1)} %get-tuple-element.7.f_ref, bf16[512,256]{1,0:T(8,128)(2,1)} %get-tuple-element.8.folded_ref), custom_call_target="tpu_custom_call" | custom-call | tf_op jit(solution)/shard_map/pallas_call | solution.py:485
